TPU v7x, 32 devices: a whole 2x2x4 slice. The times are simulated.
32 devices in a mesh: rows: 16 (over z, y, core), sub: 2 (over x).
Axes of the slice: x: 2, y: 2, z: 4, core: 2. Of those that a mesh axis runs over, the one named last changes fastest.
Arguments:
- features: bfloat16 [131072, 512], P(('rows', 'sub')), may hold values from -16 to 16
- residual: float32 [131072, 128], P(('rows', 'sub')), may hold values from -6 to 6
- coefficients: float32 [131072, 128], P(('rows', 'sub')), may hold values from -6 to 6
- block_owner: int32 [2], replicated, may hold values from 0 to 31
- block_tiles: int32 [2, 4], replicated, may hold values from 0 to 31, as said below
Outputs:
- residual_out: float32 [131072, 128], P(('rows', 'sub'))
- coefficients_out: float32 [131072, 128], P(('rows', 'sub'))
Inputs may be any that keep to these rules, and one draw needn't show every extreme that they name: `block_tiles`: in each step the tile numbers are distinct, and tiles 0 and 31 are among them.
All inputs are finite; a program needn't handle non-finite values.
Results may differ from a plain program's by a relative error of at most 0.0012.
Values may be sent and summed in bfloat16 or wider, within the bound.
No kernel may reach another device: no remote copies, remote signals or barrier semaphores. Data moves between devices by JAX's collectives and lax.ppermute only.
A program may use at most 128 MiB of HBM per device.

v0:
```python
import math

import jax
import jax.numpy as jnp
from jax import lax
from jax.sharding import PartitionSpec as P

BLOCK = 512
TILE = 128
STEPS = 2


RIDGE = 0.5


def from_root(value, axis, source):
    kept = jnp.where(lax.axis_index(axis) == source, value, 0).astype(value.dtype)
    return lax.psum(kept, axis)


def kernel_slab(left_rows, right_rows, left_norm, right_norm, kernel_scale):
    cross_dot = jnp.einsum("rf,bf->rb", left_rows, right_rows, preferred_element_type=jnp.float32)
    distance = left_norm[:, None] + right_norm[None, :] - 2.0 * cross_dot
    return jnp.exp(-kernel_scale * distance)


def block_solve(kernel_bb, gradient):
    size_now = kernel_bb.shape[0]
    system = kernel_bb + RIDGE * jnp.eye(size_now, dtype=jnp.float32)
    factor = jnp.linalg.cholesky(system)
    half_way = lax.linalg.triangular_solve(factor, gradient, left_side=True, lower=True)
    return lax.linalg.triangular_solve(
        factor, half_way, left_side=True, lower=True, transpose_a=True
    )


def fetch_block(features, owner_now, tile_ids):
    rows_dev, width = features.shape
    picked = features.reshape(rows_dev // TILE, TILE, width)[tile_ids].reshape(BLOCK, width)
    return from_root(picked, ("rows", "sub"), owner_now)


def local(features, residual, coefficients, block_owner, block_tiles):
    rows_dev, width = features.shape
    targets = residual.shape[1]
    sub_count = lax.axis_size("sub")
    devices = lax.axis_size("rows") * sub_count
    self_index = lax.axis_index("rows") * sub_count + lax.axis_index("sub")
    kernel_scale = 1.0 / width
    step_size = 1.0 / math.sqrt(rows_dev * devices)
    row_norms = jnp.einsum("rf,rf->r", features, features, preferred_element_type=jnp.float32)
    for step_index in range(STEPS):
        owner_now = block_owner[step_index]
        tile_ids = block_tiles[step_index]
        block_rows = fetch_block(features, owner_now, tile_ids)
        block_norm = jnp.einsum(
            "bf,bf->b", block_rows, block_rows, preferred_element_type=jnp.float32
        )
        slab = kernel_slab(features, block_rows, row_norms, block_norm, kernel_scale).astype(
            jnp.bfloat16
        )
        weighted = (residual - RIDGE * coefficients).astype(jnp.bfloat16)
        local_term = jnp.einsum("rb,rc->bc", slab, weighted, preferred_element_type=jnp.float32)
        gradient = lax.psum(local_term, ("rows", "sub"))
        kernel_bb = kernel_slab(block_rows, block_rows, block_norm, block_norm, kernel_scale)
        update = block_solve(kernel_bb, gradient) * step_size
        update_low = update.astype(jnp.bfloat16)
        residual = residual - jnp.dot(slab, update_low, preferred_element_type=jnp.float32)
        contribution = jnp.where(self_index == owner_now, update, jnp.zeros_like(update))
        tiled = coefficients.reshape(rows_dev // TILE, TILE, targets)
        tiled = tiled.at[tile_ids].add(contribution.reshape(BLOCK // TILE, TILE, targets))
        coefficients = tiled.reshape(rows_dev, targets)
    return (residual, coefficients)


def solution(mesh):
    in_specs = (
        P(("rows", "sub"), None),
        P(("rows", "sub"), None),
        P(("rows", "sub"), None),
        P(),
        P(),
    )
    out_specs = (P(("rows", "sub"), None), P(("rows", "sub"), None))
    return jax.shard_map(local, mesh=mesh, in_specs=in_specs, out_specs=out_specs, check_vma=False)
```

profile of v0, /device:TPU:0, one launch (start us, length us, event | category | flops | bytes accessed | tf_op | source)
XLA Modules:
  0.0 578.0 jit_solution(595273210357925339)
XLA Ops:
  9.4 2.8 gather_fusion
  12.2 2.8 gather_fusion.1
  18.0 3.1 fusion.6
  21.1 129.8 %all-reduce.10.cloned.1.call-done = (bf16[512,512]{1,0:T(8,128)(2,1)}, bf16[512,512]{1,0:T(8,128)(2,1)}) async-done(((bf16[512,512]{1,0:T(8,128)(2,1)}, bf16[512,512]{1,0:T(8,128)(2,1)}), (bf16[512,512]{1,0:T(8,128)(2,1)}, bf16[512,512]{1,0:T(8,128)(2,1)})) %all-reduce.10.cloned.1.call-update) | async-done | bytes 1048592 | tf_op jit(solution)/shard_map/psum | solution.py:18
  153.9 7.0 %fusion.5 = bf16[4096,512]{0,1:T(8,128)(2,1)} fusion(bf16[512,512]{1,0:T(8,128)(2,1)} %get-tuple-element.53, bf16[4096,512]{1,0:T(8,128)(2,1)} %param.10, f32[512]{0:T(512)S(1)} %fusion.18, f32[4096]{0:T(1024)S(1)} %fusion.6), kind=kOutput, calls=%fused_computation.15 | convolution fusion | flops 2157969408 | bytes 8931328 | tf_op jit(solution)/shard_map/rf,bf->rb/dot_general | solution.py:22
  161.1 4.6 fusion.2
  170.9 11.7 %cholesky.286 = f32[128,128]{1,0:T(8,128)S(1)} custom-call(f32[128,128]{1,0:T(8,128)S(1)} %cholesky.426), custom_call_target="Cholesky" | custom-call | tf_op jit(solution)/shard_map/jit(cholesky)/cholesky | solution.py:30
  182.8 10.0 %custom-call.31 = f32[1,128,128]{1,2,0:T(8,128)S(1)} custom-call(f32[1,128,128]{2,1,0:T(8,128)S(1)} %get-tuple-element.78), custom_call_target="InvertDiagBlocksLowerTriangular" | custom-call | tf_op jit(solution)/shard_map/jit(cholesky)/cholesky | solution.py:30
  195.3 11.7 %cholesky.305 = f32[128,128]{1,0:T(8,128)S(1)} custom-call(f32[128,128]{1,0:T(8,128)S(1)} %cholesky.430), custom_call_target="Cholesky" | custom-call | tf_op jit(solution)/shard_map/jit(cholesky)/cholesky | solution.py:30
  207.0 9.8 %custom-call.32 = f32[1,128,128]{1,2,0:T(8,128)S(1)} custom-call(f32[1,128,128]{2,1,0:T(8,128)S(1)} %get-tuple-element.75), custom_call_target="InvertDiagBlocksLowerTriangular" | custom-call | tf_op jit(solution)/shard_map/jit(cholesky)/cholesky | solution.py:30
  218.4 11.9 %cholesky.326 = f32[128,128]{1,0:T(8,128)S(1)} custom-call(f32[128,128]{1,0:T(8,128)S(1)} %cholesky.435), custom_call_target="Cholesky" | custom-call | tf_op jit(solution)/shard_map/jit(cholesky)/cholesky | solution.py:30
  230.4 9.8 %custom-call.33 = f32[1,128,128]{1,2,0:T(8,128)S(1)} custom-call(f32[1,128,128]{2,1,0:T(8,128)S(1)} %get-tuple-element.72), custom_call_target="InvertDiagBlocksLowerTriangular" | custom-call | tf_op jit(solution)/shard_map/jit(cholesky)/cholesky | solution.py:30
  241.6 11.7 %cholesky.343 = f32[128,128]{1,0:T(8,128)S(1)} custom-call(f32[128,128]{1,0:T(8,128)S(1)} %convolution_subtract_fusion.19), custom_call_target="Cholesky" | custom-call | tf_op jit(solution)/shard_map/jit(cholesky)/cholesky | solution.py:30
  256.0 4.8 fusion.14
  265.2 14.5 %while.8 = (s32[]{:T(128)}, f32[512,512]{1,0:T(8,128)}, s32[4,2]{0,1:T(2,128)S(1)}, f32[4,128,128]{2,1,0:T(8,128)}, s32[]{:T(128)}) while((s32[]{:T(128)}, f32[512,512]{1,0:T(8,128)}, s32[4,2]{0,1:T(2,128)S(1)}, f32[4,128,128]{2,1,0:T(8,128)}, s32[]{:T(128)}) %tuple.66), condition=%wide.while_cond.1, body=%wide.while_body.1.sunk | while | flops 2 | bytes 132205 | solution.py:32
  265.9 2.9 bitcast_dynamic-update-slice_fusion.4
  269.4 2.9 bitcast_dynamic-update-slice_fusion.4
  273.0 2.9 bitcast_dynamic-update-slice_fusion.4
  276.5 2.8 bitcast_dynamic-update-slice_fusion.4
  283.8 11.7 %cholesky.358 = f32[128,128]{1,0:T(8,128)S(1)} custom-call(f32[128,128]{1,0:T(8,128)S(1)} %cholesky.439), custom_call_target="Cholesky" | custom-call | tf_op jit(solution)/shard_map/jit(cholesky)/cholesky | solution.py:30
  295.6 9.8 %custom-call.36 = f32[1,128,128]{1,2,0:T(8,128)S(1)} custom-call(f32[1,128,128]{2,1,0:T(8,128)S(1)} %get-tuple-element.68), custom_call_target="InvertDiagBlocksLowerTriangular" | custom-call | tf_op jit(solution)/shard_map/jit(cholesky)/cholesky | solution.py:30
  308.0 11.7 %cholesky.377 = f32[128,128]{1,0:T(8,128)S(1)} custom-call(f32[128,128]{1,0:T(8,128)S(1)} %cholesky.443), custom_call_target="Cholesky" | custom-call | tf_op jit(solution)/shard_map/jit(cholesky)/cholesky | solution.py:30
  319.7 10.0 %custom-call.37 = f32[1,128,128]{1,2,0:T(8,128)S(1)} custom-call(f32[1,128,128]{2,1,0:T(8,128)S(1)} %get-tuple-element.65), custom_call_target="InvertDiagBlocksLowerTriangular" | custom-call | tf_op jit(solution)/shard_map/jit(cholesky)/cholesky | solution.py:30
  331.3 11.7 %cholesky.398 = f32[128,128]{1,0:T(8,128)S(1)} custom-call(f32[128,128]{1,0:T(8,128)S(1)} %cholesky.448), custom_call_target="Cholesky" | custom-call | tf_op jit(solution)/shard_map/jit(cholesky)/cholesky | solution.py:30
  343.0 9.8 %custom-call.38 = f32[1,128,128]{1,2,0:T(8,128)S(1)} custom-call(f32[1,128,128]{2,1,0:T(8,128)S(1)} %get-tuple-element.62), custom_call_target="InvertDiagBlocksLowerTriangular" | custom-call | tf_op jit(solution)/shard_map/jit(cholesky)/cholesky | solution.py:30
  354.3 11.7 %cholesky.415 = f32[128,128]{1,0:T(8,128)S(1)} custom-call(f32[128,128]{1,0:T(8,128)S(1)} %convolution_subtract_fusion.16), custom_call_target="Cholesky" | custom-call | tf_op jit(solution)/shard_map/jit(cholesky)/cholesky | solution.py:30
  372.5 40.1 %custom-call.35 = f32[4,128,128]{1,2,0:T(8,128)S(1)} custom-call(f32[4,128,128]{2,1,0:T(8,128)} %get-tuple-element.34), custom_call_target="InvertDiagBlocksLowerTriangular" | custom-call | tf_op jit(solution)/shard_map/triangular_solve/custom-call.8 | solution.py:32
  425.9 4.6 fusion.7
  432.5 7.6 %while.9 = (s32[]{:T(128)}, f32[512,512]{1,0:T(8,128)S(1)}, s32[4,2]{0,1:T(2,128)S(1)}, f32[4,128,128]{2,1,0:T(8,128)S(1)}, s32[]{:T(128)}) while((s32[]{:T(128)}, f32[512,512]{1,0:T(8,128)S(1)}, s32[4,2]{0,1:T(2,128)S(1)}, f32[4,128,128]{2,1,0:T(8,128)S(1)}, s32[]{:T(128)}) %tuple.80), condition=%wide.while_cond.1.clone, body=%wide.while_body.1.clone.sunk | while | flops 2 | bytes 131189 | solution.py:32
  440.8 40.4 %custom-call.40 = f32[4,128,128]{1,2,0:T(8,128)S(1)} custom-call(f32[4,128,128]{2,1,0:T(8,128)} %copy-done.9), custom_call_target="InvertDiagBlocksLowerTriangular" | custom-call | tf_op jit(solution)/shard_map/triangular_solve/custom-call.8 | solution.py:32
  481.2 75.9 %all-reduce.8.cloned.1.call-done = f32[512,128]{1,0:T(8,128)} async-done(((f32[512,128]{1,0:T(8,128)}), f32[512,128]{1,0:T(8,128)}) %all-reduce.8.cloned.1.call-update) | async-done | bytes 262160 | tf_op jit(solution)/shard_map/psum | solution.py:64
  564.7 4.3 convolution_subtract_fusion
  (141 shorter events, 71.9 us)
Async XLA Ops:
  7.2 1.7 copy-start.10
  7.2 1.7 copy-start.11
  7.2 143.7 %all-reduce.10.cloned.1.call-start = ((), (), s32[]{:S(2)}) async-start(), calls=%async_computation.2 | async-start | bytes 2097152 | tf_op jit(solution)/shard_map/psum | solution.py:18
  18.0 394.7 %all-reduce.6.cloned.1.call-start = ((), (), s32[]{:S(2)}) async-start(), calls=%async_computation | async-start | bytes 524288 | tf_op jit(solution)/shard_map/psum | solution.py:64
  153.9 7.0 %copy-start.8 = (bf16[512,512]{1,0:T(8,128)(2,1)S(1)}, bf16[512,512]{1,0:T(8,128)(2,1)}, u32[]{:S(2)}) copy-start(bf16[512,512]{1,0:T(8,128)(2,1)} %get-tuple-element.54) | copy-start | bytes 1572868
  153.9 7.2 %copy-start.4 = (bf16[4096,512]{1,0:T(8,128)(2,1)S(1)}, bf16[4096,512]{1,0:T(8,128)(2,1)}, u32[]{:S(2)}) copy-start(bf16[4096,512]{1,0:T(8,128)(2,1)} %param.10) | copy-start | bytes 12582916
  169.9 1.0 copy-start.6
  260.8 296.3 %all-reduce.8.cloned.1.call-start = ((), (), s32[]{:S(2)}) async-start(), calls=%async_computation.1 | async-start | bytes 524288 | tf_op jit(solution)/shard_map/psum | solution.py:64
  282.8 1.0 copy-start.7
  423.7 2.2 copy-start
  425.9 4.6 copy-start.1
  430.5 2.0 copy-start.5
  440.1 0.7 copy-start.9
  557.1 7.6 %copy-start.2 = (bf16[4096,512]{0,1:T(8,128)(2,1)S(1)}, bf16[4096,512]{0,1:T(8,128)(2,1)}, u32[]{:S(2)}) copy-start(bf16[4096,512]{0,1:T(8,128)(2,1)} %fusion.2) | copy-start | bytes 12582916
  569.7 1.3 copy-start.3
Sparse Core Ops, SparseCore 0:
  18.1 132.7 all-reduce.9
  261.0 124.9 all-reduce.5
  432.6 124.5 all-reduce.7
where the time goes:
time: 588 us; the launch traced here: 578 us
  other arithmetic  252 us (43%)
  waiting for transfers between devices  206 us (35%)
  matrix products  58.9 us (10%)
  local copies, waits for them, and re-layouts  39.3 us (7%)
  between operations  21.1 us (4%)
    another operation x30, other arithmetic, block_solve(): factor = jnp.linalg.cholesky(system)  159 us
    psum x1, waiting for transfers between devices, from_root(): return lax.psum(kept, axis)  130 us
    another operation x5, other arithmetic, block_solve(): lax.linalg.triangular_solve(factor, half_way, left_side=True, lower=True,...  82.9 us
    psum x2, waiting for transfers between devices, local(): gradient = lax.psum(local_term, ('rows', 'sub'))  76 us
    another operation x27, local copies, waits for them, and re-layouts, block_solve(): lax.linalg.triangular_solve(factor, half_way, left_side=True, lower=True,...  22.4 us
    dot_general x4, matrix products, kernel_slab(): jnp.einsum('rf,bf->rb', left_rows, right_rows, preferred_element_type=jnp...  14.8 us
  transfers between devices with their start and end apart: 3, of which 2 were waited for; matrix products, arithmetic and copies ran while one was open for 34% of the time, Pallas kernels for 0%

commit v1 on v0

v1 whole, which is shorter than its diff:
```python
import functools
import math

import jax
import jax.numpy as jnp
from jax import lax
from jax.experimental import pallas as pl
from jax.experimental.pallas import tpu as pltpu
from jax.sharding import PartitionSpec as P

BLOCK = 512
TILE = 128
STEPS = 2
RIDGE = 0.5
AXES = ("rows", "sub")
HIGH = lax.Precision.HIGHEST
NT = (((1,), (1,)), ((), ()))
LOG2E = math.log2(math.e)
VMEM_LIMIT = 24 * 1024 * 1024
SMALL_LIMIT = 12 * 1024 * 1024


def pick_kernel(tiles_ref, core_ref, feat_ref, keep_ref, send_ref, sems):
    per_half = keep_ref.shape[1] // TILE
    copies = []
    for turn, out in enumerate((keep_ref, send_ref)):
        half = core_ref[0] if turn == 0 else 1 - core_ref[0]
        for s in range(STEPS):
            for i in range(per_half):
                source = pl.multiple_of(tiles_ref[s, half * per_half + i] * TILE, TILE)
                copies.append(
                    pltpu.make_async_copy(
                        feat_ref.at[pl.ds(source, TILE), :],
                        out.at[s, pl.ds(i * TILE, TILE), :],
                        sems.at[turn, s, i],
                    )
                )
    for copy in copies:
        copy.start()
    for copy in copies:
        copy.wait()


def pick_halves(features, block_tiles, core):
    width = features.shape[1]
    half = jax.ShapeDtypeStruct((STEPS, BLOCK // 2, width), features.dtype)
    return pl.pallas_call(
        pick_kernel,
        grid_spec=pltpu.PrefetchScalarGridSpec(
            num_scalar_prefetch=2,
            grid=(1,),
            in_specs=[pl.BlockSpec(memory_space=pltpu.HBM)],
            out_specs=[pl.BlockSpec(half.shape, lambda i, *_: (0, 0, 0))] * 2,
            scratch_shapes=[pltpu.SemaphoreType.DMA((2, STEPS, BLOCK // 2 // TILE))],
        ),
        out_shape=(half, half),
        compiler_params=pltpu.CompilerParams(vmem_limit_bytes=SMALL_LIMIT),
        name="pick",
    )(block_tiles, core, pltpu.with_memory_space_constraint(features, pltpu.HBM))


def swap(value, axes, flip):
    return lax.ppermute(value, axes, [(i, i ^ flip) for i in range(lax.axis_size(axes))])


def bit_of(index, mask):
    return ((index & mask) != 0).astype(jnp.int32)


def swap_among(pick, me, axes, low, high):
    place = bit_of(me, low) + 2 * bit_of(me, high)
    flips = [0, low, high, low | high]
    return place, [swap(pick(place ^ c), axes, flips[c]) for c in (1, 2, 3)]


def ordered(parts, me, low, high, axis):
    one, two = (me & low) != 0, (me & high) != 0
    parts = [jnp.where(one, parts[c ^ 1], parts[c]) for c in range(4)]
    return jnp.stack([jnp.where(two, parts[c ^ 2], parts[c]) for c in range(4)], axis=axis)


def fetch_blocks(features, norms, block_owner, block_tiles, me, devices, core):
    width = features.shape[1]
    low, high = 1, 2 * core
    differs = lambda mask: (((block_owner ^ me) & mask) != 0)[:, None, None]
    on_core = (me & core) != 0

    keep, send = pick_halves(features, block_tiles, bit_of(me, core).reshape(1))
    half = jnp.where(differs(core), swap(send, AXES, core), keep)
    quarters = half.reshape(STEPS, 4, BLOCK // 8, width)
    pick = lambda place: lax.dynamic_index_in_dim(quarters, place, 1, False)
    place, got = swap_among(pick, me, AXES, low, high)
    part = jnp.where(
        differs(high),
        jnp.where(differs(low), got[2], got[1]),
        jnp.where(differs(low), got[0], pick(place)),
    )
    mask = 1
    while mask < devices:
        if mask not in (core, low, high):
            other = swap(part, AXES, mask)
            if mask == devices // 2:
                other, norms = lax.optimization_barrier((other, norms))
            part = jnp.where(differs(mask), other, part)
        mask *= 2
    _, got = swap_among(lambda place: part, me, AXES, low, high)
    half = ordered([part] + got, me, low, high, 1)
    other = swap(half, AXES, core)
    both = jnp.stack([jnp.where(on_core, other, half), jnp.where(on_core, half, other)], axis=1)
    return both.reshape(STEPS * BLOCK, width), norms


class Spread:
    def __init__(self, axes, core):
        self.axes, self.core = axes, core
        self.me = lax.axis_index(axes).astype(jnp.int32)
        self.near = [1 << b for b in range(3) if 1 << b != core]
        self.far = [1 << b for b in range(3, lax.axis_size(axes).bit_length() - 1)]
        self.count = 8
        self.core_axis = 2 - (core.bit_length() - 1)

    def core_sum(self, value):
        value = value.reshape((2,) * 3 + value.shape[1:])
        zero, one = (lax.index_in_dim(value, i, self.core_axis, False) for i in (0, 1))
        bit = (self.me & self.core) != 0
        value = jnp.where(bit, one, zero) + swap(jnp.where(bit, zero, one), self.axes, self.core)
        return value.reshape((4,) + value.shape[2:])

    def near_sum(self, value):
        pick = lambda place: lax.dynamic_index_in_dim(value, place, 0, False)
        place, got = swap_among(pick, self.me, self.axes, *self.near)
        return lambda got: pick(place) + got[0] + got[1] + got[2], got

    def far_sum(self, value, mask):
        return lambda got: value + got[0], [swap(value, self.axes, mask)]

    def near_gather(self, value):
        _, got = swap_among(lambda place: value, self.me, self.axes, *self.near)
        return lambda got: ordered([value] + got, self.me, *self.near, 0), got

    def core_gather(self, value):
        rest = value.shape[1:]
        value = value.reshape((2, 2) + rest)
        bit = (self.me & self.core) != 0
        got = swap(value, self.axes, self.core)
        value = jnp.stack([jnp.where(bit, got, value), jnp.where(bit, value, got)], axis=self.core_axis)
        return value.reshape((self.count,) + rest)


def scaled_norm(rows, scale):
    wide = rows.astype(jnp.float32)
    return jnp.sum(wide * wide, axis=1, keepdims=True) * scale


def gram_kernel(scale, core_ref, block_ref, own_ref, cross_ref):
    mine = block_ref[pl.ds(pl.multiple_of(core_ref[0] * BLOCK, BLOCK), BLOCK), :]
    eye = jnp.where(
        lax.broadcasted_iota(jnp.int32, (BLOCK, BLOCK), 0)
        == lax.broadcasted_iota(jnp.int32, (BLOCK, BLOCK), 1),
        RIDGE,
        0.0,
    )
    for left, right, shift, out in (
        (mine, mine, eye, own_ref),
        (block_ref[:BLOCK], block_ref[BLOCK:], 0.0, cross_ref),
    ):
        dots = lax.dot_general(left, right, NT, preferred_element_type=jnp.float32)
        right_norm = scaled_norm(right, scale)
        row = jnp.transpose(jnp.broadcast_to(right_norm, (BLOCK, 128)))[:1]
        value = jnp.exp(dots * (2.0 * scale) - scaled_norm(left, scale) - row)
        out[...] = (value + shift).astype(out.dtype)


def gram(block, core, scale):
    square = (BLOCK, BLOCK)
    whole = lambda shape: pl.BlockSpec(shape, lambda i, *_: (0, 0))
    return pl.pallas_call(
        functools.partial(gram_kernel, scale),
        grid_spec=pltpu.PrefetchScalarGridSpec(
            num_scalar_prefetch=1,
            grid=(1,),
            in_specs=[whole(block.shape)],
            out_specs=[whole(square)] * 2,
        ),
        out_shape=(jax.ShapeDtypeStruct(square, jnp.float32), jax.ShapeDtypeStruct(square, jnp.bfloat16)),
        compiler_params=pltpu.CompilerParams(vmem_limit_bytes=SMALL_LIMIT),
        cost_estimate=pl.CostEstimate(
            flops=2 * 2 * BLOCK**3, bytes_accessed=4 * BLOCK * BLOCK * 4, transcendentals=2 * BLOCK**2
        ),
        name="gram",
    )(core, block)


def slab_kernel(scale, chunk, block_ref, feat_ref, norm_ref, res_ref, coef_ref, slab_ref, piece_ref, bnorm, grad, cross):
    scale2 = scale * LOG2E
    norm = scaled_norm(block_ref[...], scale2)
    bnorm[...] = jnp.broadcast_to(norm, bnorm.shape)
    grad[...] = jnp.zeros_like(grad)
    cross[...] = jnp.zeros_like(cross)
    part = BLOCK // 2

    def body(i, _):
        rows = pl.ds(pl.multiple_of(i * chunk, chunk), chunk)
        weighted = (res_ref[rows, :] - RIDGE * coef_ref[rows, :]).astype(jnp.bfloat16)
        feat = feat_ref[rows, :]
        norm_row = norm_ref[:, rows] * LOG2E
        for p in range(STEPS * 2):
            at = slice(p * part, (p + 1) * part)
            dots = lax.dot_general(block_ref[at], feat, NT, preferred_element_type=jnp.float32)
            norm_wide = jnp.concatenate([bnorm[at]] * (chunk // bnorm.shape[1]), axis=1)
            slab = jnp.exp2(dots * (2.0 * scale2) - norm_wide - norm_row).astype(jnp.bfloat16)
            slab_ref[at, rows] = slab
            grad[at] += jnp.dot(slab, weighted, preferred_element_type=jnp.float32)
        cross[...] += lax.dot_general(
            slab_ref[:BLOCK, rows], slab_ref[BLOCK:, rows], NT, preferred_element_type=jnp.float32
        )
        return 0

    lax.fori_loop(0, feat_ref.shape[0] // chunk, body, 0)
    grads = jnp.transpose(grad[...])
    groups = piece_ref.shape[0]
    own, depth = grads.shape[0] // groups, BLOCK // groups
    for d in range(groups):
        for s in range(STEPS):
            piece_ref[d, s * own : (s + 1) * own] = grads[d * own : (d + 1) * own, s * BLOCK : (s + 1) * BLOCK]
        piece_ref[d, STEPS * own :] = cross[d * depth : (d + 1) * depth]


def in_vmem(value):
    return pltpu.with_memory_space_constraint(value, pltpu.VMEM)


def slabs(block, features, norms, residual, coefficients, scale, groups, chunk=512):
    rows, width = features.shape
    targets = residual.shape[1]
    both = STEPS * BLOCK
    piece = (groups, STEPS * targets // groups + BLOCK // groups, BLOCK)
    return pl.pallas_call(
        functools.partial(slab_kernel, scale, chunk),
        out_shape=(pltpu.VMEM((both, rows), jnp.bfloat16), jax.ShapeDtypeStruct(piece, jnp.float32)),
        scratch_shapes=[
            pltpu.VMEM((both, 128), jnp.float32),
            pltpu.VMEM((both, targets), jnp.float32),
            pltpu.VMEM((BLOCK, BLOCK), jnp.float32),
        ],
        compiler_params=pltpu.CompilerParams(vmem_limit_bytes=VMEM_LIMIT),
        cost_estimate=pl.CostEstimate(
            flops=2 * rows * both * (width + targets + BLOCK // 2),
            bytes_accessed=rows * (width * 2 + targets * 8 + both * 2),
            transcendentals=rows * both,
        ),
        name="slabs",
    )(block, in_vmem(features), norms, in_vmem(residual), in_vmem(coefficients))


def reciprocal(x):
    guess = pl.reciprocal(x, approx=True)
    return guess * (2.0 - x * guess)


def eliminate(tiles, t, lane, scaled_ref):
    start, shape = 8 * t, tiles[t].shape
    wide = lambda tile, k: jnp.broadcast_to(tile[:, start + k : start + k + 1], shape)
    rows = [jnp.broadcast_to(tiles[t][k : k + 1], shape) for k in range(8)]
    at = {(i, k): wide(rows[i], k) for i in range(8) for k in range(i, 8)}
    units = [jnp.where(lane == start + k, 1.0, 0.0) for k in range(8)]
    rows = [row + unit for row, unit in zip(rows, units)]
    total, lower = [None] * 8, {}
    for r in range(0, 8, 2):
        p, m, q = at[r, r], at[r, r + 1], at[r + 1, r + 1]
        inverse = reciprocal(p * q - m * m)
        p, m, q = p * inverse, m * inverse, q * inverse
        for k in range(r + 2, 8):
            first = q * at[r, k] - m * at[r + 1, k]
            second = p * at[r + 1, k] - m * at[r, k]
            lower[r, k], lower[r + 1, k] = first, second
            for i in range(r + 2, k + 1):
                at[i, k] = at[i, k] - (at[r, i] * first + at[r + 1, i] * second)
            rows[k] = rows[k] - (first * rows[r] + second * rows[r + 1])
        total[r] = q * rows[r] - m * rows[r + 1]
        total[r + 1] = p * rows[r + 1] - m * rows[r]
    for r in (4, 2, 0):
        for k in range(r + 2, 8):
            total[r] = total[r] - lower[r, k] * total[k]
            total[r + 1] = total[r + 1] - lower[r + 1, k] * total[k]
    for k in range(8):
        scaled_ref[start + k : start + k + 1] = total[k][:1] - units[k][:1]
    for u in range(t + 1, len(tiles)):
        parts = [wide(tiles[u], k) * total[k] for k in range(8)]
        while len(parts) > 1:
            parts = [x + y for x, y in zip(parts[::2], parts[1::2])]
        tiles[u] = tiles[u] - parts[0]


def factor_kernel(index, copies, *refs):
    refs = list(refs)
    rest_ref = refs.pop(0)
    if copies:
        source, scaled, sem = refs.pop(0), refs[-2], refs[-1]
        copy = pltpu.make_async_copy(source, refs[-3], sem)
        copy.start()
    else:
        scaled = refs[-1]
    last = rest_ref.shape[0] == TILE
    factor_ref = refs[0] if last else refs[1]
    here = slice(index * TILE, (index + 1) * TILE)
    row_ids = lax.broadcasted_iota(jnp.int32, (TILE, TILE), 0)
    col_ids = lax.broadcasted_iota(jnp.int32, (TILE, TILE), 1)
    lane = lax.broadcasted_iota(jnp.int32, (8, TILE), 1)
    tiles = [rest_ref[8 * t : 8 * t + 8, here] for t in range(TILE // 8)]
    for t in range(TILE // 8):
        eliminate(tiles, t, lane, scaled)
    start = row_ids - row_ids % 8
    dot = functools.partial(lax.dot_general, precision=HIGH, preferred_element_type=jnp.float32)
    lower = jnp.where(col_ids < start, jnp.concatenate(tiles, axis=0), 0.0)
    lower = lower + jnp.where(col_ids == row_ids, 1.0, 0.0)
    right = jnp.where(col_ids < start + 8, scaled[...], 0.0)
    inv = dot(lower, right, (((0,), (0,)), ((), ())))
    top = rest_ref[:TILE]
    panel = dot(inv, top, (((1,), (0,)), ((), ())))
    inside = lax.broadcasted_iota(jnp.int32, panel.shape, 1) // TILE == index
    panel = jnp.where(inside, jnp.concatenate([inv] * (BLOCK // TILE), axis=1), panel)
    factor_ref[:TILE] = top
    factor_ref[TILE:] = panel
    if not last:
        under = rest_ref[TILE:]
        change = dot(rest_ref[TILE:, here], panel, (((1,), (0,)), ((), ())))
        inside = lax.broadcasted_iota(jnp.int32, under.shape, 1) // TILE == index
        refs[0][...] = jnp.where(inside, 0.0, under) - change
    if copies:
        copy.wait()


def factor_step(rest, index, copied=None):
    left = rest.shape[0] - TILE
    vmem, hbm = pl.BlockSpec(memory_space=pltpu.VMEM), pl.BlockSpec(memory_space=pltpu.HBM)
    out = [jax.ShapeDtypeStruct((left, BLOCK), jnp.float32)] if left else []
    out.append(jax.ShapeDtypeStruct((2 * TILE, BLOCK), jnp.float32))
    inputs, in_specs, out_specs = [rest], [vmem], [vmem] * len(out)
    scratch = [pltpu.VMEM((TILE, TILE), jnp.float32)]
    if copied is not None:
        inputs.append(pltpu.with_memory_space_constraint(copied, pltpu.HBM))
        in_specs.append(hbm)
        out.append(pltpu.HBM(copied.shape, copied.dtype))
        out_specs.append(hbm)
        scratch.append(pltpu.SemaphoreType.DMA)
    out = pl.pallas_call(
        functools.partial(factor_kernel, index, copied is not None),
        in_specs=in_specs,
        out_specs=tuple(out_specs),
        out_shape=tuple(out),
        scratch_shapes=scratch,
        compiler_params=pltpu.CompilerParams(vmem_limit_bytes=SMALL_LIMIT),
        cost_estimate=pl.CostEstimate(flops=6 * 10**9, bytes_accessed=4 * 1024 * 1024, transcendentals=0),
        name="factor",
    )(*inputs)
    out = list(out)
    below = out.pop(0) if left else None
    return (below,) + tuple(out)


def apply_inverse(value, refs):
    ids = lambda axis: lax.broadcasted_iota(jnp.int32, (TILE, BLOCK), axis)
    lower, right = [], []
    for k in range(BLOCK // TILE):
        rest, panel = refs[k][:TILE], refs[k][TILE:]
        unit = jnp.where(ids(1) == ids(0) + k * TILE, 1.0, 0.0)
        lower.append(jnp.where(ids(1) < k * TILE, rest, unit))
        right.append(jnp.where(ids(1) < (k + 1) * TILE, panel, 0.0))
    lower, right = jnp.concatenate(lower, axis=0), jnp.concatenate(right, axis=0)
    middle = lax.dot_general(value, right, NT, precision=HIGH, preferred_element_type=jnp.float32)
    return jnp.dot(middle, lower, precision=HIGH, preferred_element_type=jnp.float32)


def first_kernel(step_size, grad_ref, *refs):
    refs[-1][...] = apply_inverse(grad_ref[: refs[-1].shape[0]], refs[:-1]) * step_size


def second_kernel(step_size, grad_ref, first_ref, cross_ref, gram_ref, *refs):
    out_ref = refs[-1]
    first = first_ref[...]
    own = first.shape[0]
    again = (
        grad_ref[own:]
        - jnp.dot(first.astype(jnp.bfloat16), cross_ref[...], preferred_element_type=jnp.float32)
        - RIDGE * jnp.dot(first, gram_ref[...].astype(jnp.float32), precision=HIGH, preferred_element_type=jnp.float32)
    )
    out_ref[:own] = first.astype(out_ref.dtype)
    out_ref[own:] = (apply_inverse(again, refs[:-1]) * step_size).astype(out_ref.dtype)


def solve(kernel, out, arrays, factors, step_size):
    whole = lambda value: pl.BlockSpec(value.shape, lambda i: (0,) * len(value.shape))
    return pl.pallas_call(
        functools.partial(kernel, step_size),
        grid=(1,),
        in_specs=[whole(value) for value in list(arrays) + list(factors)],
        out_specs=whole(out),
        out_shape=out,
        compiler_params=pltpu.CompilerParams(vmem_limit_bytes=SMALL_LIMIT),
        cost_estimate=pl.CostEstimate(flops=10**9, bytes_accessed=3 * 1024 * 1024, transcendentals=0),
        name=kernel.__name__[:-7],
    )(*arrays, *factors)


def final_kernel(chunk, owner_ref, tiles_ref, me_ref, gathered_ref, slab_ref, res_ref, coef_ref, base_ref, res_out, coef_out, upd_ref, res_buf, tile_buf, res_sems, tile_sems):
    rows, targets = res_ref.shape
    groups, own2 = gathered_ref.shape[0], gathered_ref.shape[1]
    own = own2 // STEPS
    count = BLOCK // TILE
    flat = gathered_ref[...].reshape(groups * own2, BLOCK)
    target = lax.broadcasted_iota(jnp.int32, (targets, groups * own2), 0)
    place = lax.broadcasted_iota(jnp.int32, (targets, groups * own2), 1)
    wanted = target // own * own2 + target % own
    for s in range(STEPS):
        pick = jnp.where(place == wanted + s * own, 1.0, 0.0).astype(jnp.bfloat16)
        chosen = jnp.dot(pick, flat, preferred_element_type=jnp.float32)
        upd_ref[:, s * BLOCK : (s + 1) * BLOCK] = chosen.astype(jnp.bfloat16)

    def change_of(s, k):
        at = s * BLOCK + k * TILE
        return jnp.transpose(upd_ref[:, at : at + TILE].astype(jnp.float32))

    def tile_rows(s, k):
        return pl.ds(pl.multiple_of(tiles_ref[s, k] * TILE, TILE), TILE)

    def tile_copy(s, k):
        return pltpu.make_async_copy(tile_buf.at[s, k], coef_out.at[tile_rows(s, k), :], tile_sems.at[s, k])

    owned = [owner_ref[s] == me_ref[0] for s in range(STEPS)]

    def writes(s, k):
        kept = owned[s]
        for later in range(s + 1, STEPS):
            for j in range(count):
                kept = kept & jnp.logical_not(owned[later] & (tiles_ref[later, j] == tiles_ref[s, k]))
        return kept

    for s in range(STEPS):
        for k in range(count):

            @pl.when(writes(s, k))
            def _():
                tile_buf[s, k] = coef_ref[tile_rows(s, k), :] + change_of(s, k)
                for earlier in range(s):
                    for j in range(count):

                        @pl.when(owned[earlier] & (tiles_ref[earlier, j] == tiles_ref[s, k]))
                        def _():
                            tile_buf[s, k] += change_of(earlier, j)

                tile_copy(s, k).start()

    def res_copy(i):
        at = pl.ds(pl.multiple_of(i * chunk, chunk), chunk)
        return pltpu.make_async_copy(res_buf.at[at, :], res_out.at[at, :], res_sems.at[i])

    def body(i, _):
        at = pl.ds(pl.multiple_of(i * chunk, chunk), chunk)
        change = jnp.dot(upd_ref[...], slab_ref[:, at], preferred_element_type=jnp.float32)
        res_buf[at, :] = res_ref[at, :] - jnp.transpose(change)
        res_copy(i).start()
        return 0

    lax.fori_loop(0, rows // chunk, body, 0)
    for i in range(rows // chunk):
        res_copy(i).wait()
    for s in range(STEPS):
        for k in range(count):

            @pl.when(writes(s, k))
            def _():
                tile_copy(s, k).wait()


def finish(owner, tiles, me, gathered, slab, residual, coefficients, base, chunk=512):
    rows, targets = residual.shape
    both = STEPS * BLOCK
    count = BLOCK // TILE
    smem, vmem, hbm = (pl.BlockSpec(memory_space=space) for space in (pltpu.SMEM, pltpu.VMEM, pltpu.HBM))
    return pl.pallas_call(
        functools.partial(final_kernel, chunk),
        in_specs=[smem] * 3 + [vmem] * 4 + [hbm],
        out_specs=(hbm, hbm),
        out_shape=(
            pltpu.HBM(residual.shape, jnp.float32),
            pltpu.HBM(residual.shape, jnp.float32),
        ),
        scratch_shapes=[
            pltpu.VMEM((targets, both), jnp.bfloat16),
            pltpu.VMEM((rows, targets), jnp.float32),
            pltpu.VMEM((STEPS, count, TILE, targets), jnp.float32),
            pltpu.SemaphoreType.DMA((rows // chunk,)),
            pltpu.SemaphoreType.DMA((STEPS, count)),
        ],
        input_output_aliases={7: 1},
        compiler_params=pltpu.CompilerParams(vmem_limit_bytes=VMEM_LIMIT),
        cost_estimate=pl.CostEstimate(
            flops=2 * rows * both * targets, bytes_accessed=rows * (both * 2 + targets * 16), transcendentals=0
        ),
        name="finish",
    )(owner, tiles, me, gathered, in_vmem(slab), in_vmem(residual), in_vmem(coefficients), base)


def local(features, residual, coefficients, block_owner, block_tiles):
    rows_dev, width = features.shape
    targets = residual.shape[1]
    sub_count = lax.axis_size("sub")
    devices = lax.axis_size("rows") * sub_count
    me = lax.axis_index(AXES).astype(jnp.int32)
    scale = 1.0 / width
    step_size = 1.0 / math.sqrt(rows_dev * devices)
    spread = Spread(AXES, sub_count) if devices <= 32 else Spread(("rows",), 1)
    groups = spread.count
    own = targets // groups

    wide = features.astype(jnp.float32)
    norms = (jnp.sum(wide * wide, axis=1) * scale).reshape(1, rows_dev)
    block, norms = fetch_blocks(features, norms, block_owner, block_tiles, me, devices, sub_count)
    slab, pieces = slabs(block, features, norms, residual, coefficients, scale, groups)
    if spread.axes != AXES:
        pieces = lax.psum(pieces, "sub")
    core = bit_of(me, sub_count)
    rest, gram12 = gram(block, core.reshape(1), scale)
    factors, base = ([], []), None

    def beside(hop, index, rest):
        then, got = hop
        below, mine, *copied = factor_step(rest, index, coefficients if index == 0 else None)
        got, below, mine = lax.optimization_barrier((got, below, mine))
        other = swap(mine, AXES, sub_count)
        factors[0].append(jnp.where(core != 0, other, mine))
        factors[1].append(jnp.where(core != 0, mine, other))
        return then(got), below, copied

    value = spread.core_sum(pieces)
    value, rest, (base,) = beside(spread.near_sum(value), 0, rest)
    for index, mask in enumerate(spread.far):
        value, rest, _ = beside(spread.far_sum(value, mask), 1 + index, rest)
    cross = value[STEPS * own :].astype(jnp.bfloat16)
    cross, rest, _ = beside(spread.near_gather(cross), 3, rest)
    cross = spread.core_gather(cross)
    grads = value[: STEPS * own]
    first = jax.ShapeDtypeStruct((own, BLOCK), jnp.float32)
    first = solve(first_kernel, first, [grads], factors[0], step_size)
    cross, first = lax.optimization_barrier((cross, first))
    update = jax.ShapeDtypeStruct(grads.shape, jnp.bfloat16)
    update = solve(
        second_kernel, update, [grads, first, cross.reshape(BLOCK, BLOCK), gram12], factors[1], step_size
    )
    then, got = spread.near_gather(update)
    gathered = spread.core_gather(then(got))
    return finish(block_owner, block_tiles, me.reshape(1), gathered, slab, residual, coefficients, base)


def solution(mesh):
    row_spec = P(AXES, None)
    return jax.shard_map(
        local,
        mesh=mesh,
        in_specs=(row_spec, row_spec, row_spec, P(), P()),
        out_specs=(row_spec, row_spec),
        check_vma=False,
    )
```

time: 588 us -> 181 us (0.31); the launches traced: 578 us -> 181 us
  other arithmetic: 252 us -> 6.28 us
  waiting for transfers between devices: 206 us -> 31.1 us
  Pallas kernels: 0 us -> 108 us
  matrix products: 58.9 us -> 0 us
  local copies, waits for them, and re-layouts: 39.3 us -> 4.67 us
  starting transfers between devices: 0.12 us -> 29.7 us
  between operations: 21.1 us -> 1.34 us
    another operation x35 -> x12, other arithmetic: 241 us -> 0.55 us  [the longest x6 0.22 us: ordered(): jnp.stack([jnp.where(two, parts[c ^ 2], parts[c]) for c in range(4)], axi...]
    psum x3 -> x0, waiting for transfers between devices: 206 us -> none  [the longest x1 130 us: from_root(): return lax.psum(kept, axis)]
    pallas_call x0 -> x10, Pallas kernels: none -> 108 us  [the longest x4 83 us: factor_step(): pl.pallas_call(functools.partial(factor_kernel, index, copied is not None...]
    ppermute x0 -> x28, waiting for transfers between devices: none -> 31.1 us  [swap(): lax.ppermute(value, axes, [(i, i ^ flip) for i in range(lax.axis_size(axe...]
    dot_general x8 -> x0, matrix products: 30.4 us -> none  [the longest x4 14.8 us: kernel_slab(): jnp.einsum('rf,bf->rb', left_rows, right_rows, preferred_element_type=jnp...]
    ppermute x0 -> x28, starting transfers between devices: none -> 29.7 us  [swap(): lax.ppermute(value, axes, [(i, i ^ flip) for i in range(lax.axis_size(axe...]
    another operation x40 -> x0, matrix products: 28.5 us -> none  [the longest x12 10.9 us: block_solve(): factor = jnp.linalg.cholesky(system)]
    another operation x35 -> x1, local copies, waits for them, and re-layouts: 22.7 us -> 0.04 us  [core_gather(): jnp.stack([jnp.where(bit, got, value), jnp.where(bit, value, got)], axis=...]
  transfers between devices with their start and end apart: 3 -> 28, of which waited for: 2 -> 17; matrix products, arithmetic and copies ran while one was open for 34% -> 2% of each run, Pallas kernels for 0% -> 46%
where the time goes in v1:
time: 181 us
  Pallas kernels  108 us (60%)
  waiting for transfers between devices  31.1 us (17%)
  starting transfers between devices  29.7 us (16%)
  other arithmetic  6.28 us (3%)
  local copies, waits for them, and re-layouts  4.67 us (3%)
    pallas_call x4, Pallas kernels, factor_step(): pl.pallas_call(functools.partial(factor_kernel, index, copied is not None...  83 us
    ppermute x28, waiting for transfers between devices, swap(): lax.ppermute(value, axes, [(i, i ^ flip) for i in range(lax.axis_size(axe...  31.1 us
    ppermute x28, starting transfers between devices, swap(): lax.ppermute(value, axes, [(i, i ^ flip) for i in range(lax.axis_size(axe...  29.7 us
    pallas_call x1, Pallas kernels, slabs(): pl.pallas_call(functools.partial(slab_kernel, scale, chunk), out_shape=(p...  14 us
    pallas_call x1, Pallas kernels, finish(): pl.pallas_call(functools.partial(final_kernel, chunk), in_specs=[smem] *...  5.44 us
    unnamed x22, local copies, waits for them, and re-layouts  4.53 us
  transfers between devices with their start and end apart: 28, of which 17 were waited for; matrix products, arithmetic and copies ran while one was open for 2% of the time, Pallas kernels for 46%

profile of v1, /device:TPU:0, one launch (start us, length us, event | category | flops | bytes accessed | tf_op | source)
XLA Modules:
  0.0 181.4 jit_solution(16446593888145358859)
XLA Ops:
  1.3 1.9 %pick.1 = (bf16[2,256,512]{2,1,0:T(8,128)(2,1)S(1)}, bf16[2,256,512]{2,1,0:T(8,128)(2,1)S(1)}) custom-call(s32[2,4]{1,0:T(2,128)S(1)} %copy-done.6, s32[1]{0:T(128)} %bitcast.1.core_ref, bf16[4096,512]{1,0:T(8,128)(2,1)} %feat_ref.3), custom_call_target="tpu_custom_call" | custom-call | tf_op jit(solution)/shard_map/pick/pallas_call | solution.py:47
  3.8 1.5 collective-permute-done
  5.5 3.9 %collective-permute-start.1 = (bf16[2,64,512]{2,1,0:T(8,128)(2,1)S(1)}, bf16[2,64,512]{2,1,0:T(8,128)(2,1)S(1)}, u32[]{:S(2)}, u32[]{:S(2)}) collective-permute-start(bf16[2,64,512]{2,1,0:T(8,128)(2,1)S(1)} %get-tuple-element.89), channel_id=1, source_target_pairs={{0,5},{1,4},{2,7},{3,6},{4,1},{5,0},{6,3},{7,2},{8,13},{9,12},{10,... | collective-permute-start | bytes 393224 | tf_op jit(solution)/shard_map/ppermute | solution.py:63
  10.0 3.3 %collective-permute-done.1 = bf16[2,64,512]{2,1,0:T(8,128)(2,1)S(1)} collective-permute-done((bf16[2,64,512]{2,1,0:T(8,128)(2,1)S(1)}, bf16[2,64,512]{2,1,0:T(8,128)(2,1)S(1)}, u32[]{:S(2)}, u32[]{:S(2)}) %collective-permute-start.1) | collective-permute-done | bytes 131104 | tf_op jit(solution)/shard_map/ppermute | solution.py:63
  13.2 2.7 %collective-permute-done.2 = bf16[2,64,512]{2,1,0:T(8,128)(2,1)S(1)} collective-permute-done((bf16[2,64,512]{2,1,0:T(8,128)(2,1)S(1)}, bf16[2,64,512]{2,1,0:T(8,128)(2,1)S(1)}, u32[]{:S(2)}, u32[]{:S(2)}) %collective-permute-start.2) | collective-permute-done | bytes 131104 | tf_op jit(solution)/shard_map/ppermute | solution.py:63
  16.3 1.6 collective-permute-start.4
  18.0 3.2 %multiply_reduce_fusion = f32[4096]{0:T(1024)S(1)} fusion(bf16[4096,512]{1,0:T(8,128)(2,1)} %feat_ref.3), kind=kLoop, calls=%fused_computation | loop fusion | flops 6287360 | bytes 4210688 | tf_op jit(solution)/shard_map/reduce_sum | solution.py:518
  21.6 2.8 %collective-permute-start.5 = (bf16[2,64,512]{2,1,0:T(8,128)(2,1)S(1)}, bf16[2,64,512]{2,1,0:T(8,128)(2,1)S(1)}, u32[]{:S(2)}, u32[]{:S(2)}) collective-permute-start(bf16[2,64,512]{2,1,0:T(8,128)(2,1)S(1)} %broadcast_select_fusion.9), channel_id=1, source_target_pairs={{0,16},{1,17},{2,18},{3,19},{4,20},{5,21},{6,22},{7,23},{8,24},{9,... | collective-permute-start | bytes 393224 | tf_op jit(solution)/shard_map/ppermute | solution.py:63
  24.5 5.7 %collective-permute-done.5 = bf16[2,64,512]{2,1,0:T(8,128)(2,1)S(1)} collective-permute-done((bf16[2,64,512]{2,1,0:T(8,128)(2,1)S(1)}, bf16[2,64,512]{2,1,0:T(8,128)(2,1)S(1)}, u32[]{:S(2)}, u32[]{:S(2)}) %collective-permute-start.5) | collective-permute-done | bytes 131104 | tf_op jit(solution)/shard_map/ppermute | solution.py:63
  31.3 1.9 %collective-permute-start.7 = (bf16[2,64,512]{2,1,0:T(8,128)(2,1)S(1)}, bf16[2,64,512]{2,1,0:T(8,128)(2,1)S(1)}, u32[]{:S(2)}, u32[]{:S(2)}) collective-permute-start(bf16[2,64,512]{2,1,0:T(8,128)(2,1)S(1)} %broadcast_select_fusion.10), channel_id=1, source_target_pairs={{0,4},{1,5},{2,6},{3,7},{4,0},{5,1},{6,2},{7,3},{8,12},{9,13},{10,... | collective-permute-start | bytes 393224 | tf_op jit(solution)/shard_map/ppermute | solution.py:63
  33.8 3.4 %collective-permute-done.6 = bf16[2,64,512]{2,1,0:T(8,128)(2,1)S(1)} collective-permute-done((bf16[2,64,512]{2,1,0:T(8,128)(2,1)S(1)}, bf16[2,64,512]{2,1,0:T(8,128)(2,1)S(1)}, u32[]{:S(2)}, u32[]{:S(2)}) %collective-permute-start.6) | collective-permute-done | bytes 131104 | tf_op jit(solution)/shard_map/ppermute | solution.py:63
  38.7 1.9 %collective-permute-done.9 = bf16[2,4,64,512]{3,2,1,0:T(8,128)(2,1)S(1)} collective-permute-done((bf16[2,4,64,512]{3,2,1,0:T(8,128)(2,1)S(1)}, bf16[2,4,64,512]{3,2,1,0:T(8,128)(2,1)S(1)}, u32[]{:S(2)}, u32[]{:S(2)}) %collective-permute-start.9) | collective-permute-done | bytes 524320 | tf_op jit(solution)/shard_map/ppermute | solution.py:63
  41.4 14.0 %slabs.1 = (bf16[1024,4096]{1,0:T(8,128)(2,1)S(1)}, f32[8,96,512]{2,1,0:T(8,128)S(1)}) custom-call(bf16[1024,512]{1,0:T(8,128)(2,1)S(1)} %bitcast.103, bf16[4096,512]{1,0:T(8,128)(2,1)S(1)} %copy-done, f32[1,4096]{1,0:T(1,128)S(1)} %bitcast.106, f32[4096,128]{1,0:T(8,128)S(1)} %copy-done.2, f32[4096,128]{1,0:T(8,128)S(1)} %copy-done.4), custom_call_target="tpu_custom_call" | custom-call | flops 7516192768 | bytes 16777216 | tf_op jit(solution)/shard_map/slabs/pallas_call | solution.py:238
  55.4 3.3 %copy-done.1 = bf16[1024,4096]{1,0:T(8,128)(2,1)} copy-done((bf16[1024,4096]{1,0:T(8,128)(2,1)}, bf16[1024,4096]{1,0:T(8,128)(2,1)S(1)}, u32[]{:S(2)}) %copy-start.1) | copy-done | bytes 8388632
  59.9 1.4 collective-permute-done.10
  61.3 1.4 fusion.1
  62.7 1.5 collective-permute-start.11
  64.8 1.5 collective-permute-start.13
  66.3 64.6 %factor.4 = (f32[384,512]{1,0:T(8,128)S(1)}, f32[256,512]{1,0:T(8,128)S(1)}, f32[4096,128]{1,0:T(8,128)}) custom-call(f32[512,512]{1,0:T(8,128)S(1)} %get-tuple-element.39.refs_0_, f32[4096,128]{1,0:T(8,128)} %coef_ref.3), custom_call_target="tpu_custom_call" | custom-call | flops 6000000000 | bytes 4194304 | tf_op jit(solution)/shard_map/factor/pallas_call | solution.py:347
  132.4 6.3 %factor.5 = (f32[256,512]{1,0:T(8,128)S(1)}, f32[256,512]{1,0:T(8,128)S(1)}) custom-call(f32[384,512]{1,0:T(8,128)S(1)} %get-tuple-element.45.refs_0_), custom_call_target="tpu_custom_call" | custom-call | flops 6000000000 | bytes 4194304 | tf_op jit(solution)/shard_map/factor/pallas_call | solution.py:347
  138.9 3.4 %collective-permute-start.15 = (f32[96,512]{1,0:T(8,128)S(1)}, f32[96,512]{1,0:T(8,128)S(1)}, u32[]{:S(2)}, u32[]{:S(2)}) collective-permute-start(f32[96,512]{1,0:T(8,128)S(1)} %add.54), channel_id=1, source_target_pairs={{0,16},{1,17},{2,18},{3,19},{4,20},{5,21},{6,22},{7,23},{8,24},{9,... | collective-permute-start | bytes 589832 | tf_op jit(solution)/shard_map/ppermute | solution.py:63
  142.3 6.3 %factor.6 = (f32[128,512]{1,0:T(8,128)S(1)}, f32[256,512]{1,0:T(8,128)S(1)}) custom-call(f32[256,512]{1,0:T(8,128)S(1)} %get-tuple-element.49.refs_0_), custom_call_target="tpu_custom_call" | custom-call | flops 6000000000 | bytes 4194304 | tf_op jit(solution)/shard_map/factor/pallas_call | solution.py:347
  148.9 2.6 %collective-permute-done.15 = f32[96,512]{1,0:T(8,128)S(1)} collective-permute-done((f32[96,512]{1,0:T(8,128)S(1)}, f32[96,512]{1,0:T(8,128)S(1)}, u32[]{:S(2)}, u32[]{:S(2)}) %collective-permute-start.15) | collective-permute-done | bytes 196640 | tf_op jit(solution)/shard_map/ppermute | solution.py:63
  151.6 1.5 collective-permute-start.16
  153.6 1.5 collective-permute-start.18
  155.1 5.8 %factor.7 = f32[256,512]{1,0:T(8,128)S(1)} custom-call(f32[128,512]{1,0:T(8,128)S(1)} %get-tuple-element.53.refs_0_), custom_call_target="tpu_custom_call" | custom-call | flops 6000000000 | bytes 4194304 | tf_op jit(solution)/shard_map/factor/pallas_call | solution.py:347
  162.0 2.0 %collective-permute-done.19 = bf16[2,2,64,512]{3,2,1,0:T(8,128)(2,1)S(1)} collective-permute-done((bf16[2,2,64,512]{3,2,1,0:T(8,128)(2,1)S(1)}, bf16[2,2,64,512]{3,2,1,0:T(8,128)(2,1)S(1)}, u32[]{:S(2)}, u32[]{:S(2)}) %collective-permute-start.19) | collective-permute-done | bytes 262176 | tf_op jit(solution)/shard_map/ppermute | solution.py:63
  165.7 1.7 second.1
  167.4 1.4 collective-permute-start.24
  168.8 1.5 collective-permute-start.25
  172.8 1.5 collective-permute-done.26
  175.8 5.4 %finish.1 = (f32[4096,128]{1,0:T(8,128)}, f32[4096,128]{1,0:T(8,128)}) custom-call(s32[2]{0:T(128)S(1)} %copy-done.8, s32[2,4]{1,0:T(2,128)S(1)} %copy-done.7, s32[1]{0:T(128)} %bitcast.me_ref, bf16[8,32,512]{2,1,0:T(8,128)(2,1)S(1)} %bitcast.102, bf16[1024,4096]{1,0:T(8,128)(2,1)S(1)} %bitcast.99, ...), custom_call_target="tpu_custom_call", output_to_operand_aliasing={{1}: (7, {})} | custom-call | flops 1073741824 | bytes 16777216 | tf_op jit(solution)/shard_map/finish/pallas_call | solution.py:481
  (91 shorter events, 17.6 us)
Async XLA Ops:
  3.2 2.1 %collective-permute-start = (bf16[2,256,512]{2,1,0:T(8,128)(2,1)S(1)}, bf16[2,256,512]{2,1,0:T(8,128)(2,1)S(1)}, u32[]{:S(2)}, u32[]{:S(2)}) collective-permute-start(bf16[2,256,512]{2,1,0:T(8,128)(2,1)S(1)} %get-tuple-element.34), channel_id=1, source_target_pairs={{0,2},{1,3},{2,0},{3,1},{4,6},{5,7},{6,4},{7,5},{8,10},{9,11},{10,... | collective-permute-start | bytes 1572872 | tf_op jit(solution)/shard_map/ppermute | solution.py:63
  5.5 7.8 %collective-permute-start.1 = (bf16[2,64,512]{2,1,0:T(8,128)(2,1)S(1)}, bf16[2,64,512]{2,1,0:T(8,128)(2,1)S(1)}, u32[]{:S(2)}, u32[]{:S(2)}) collective-permute-start(bf16[2,64,512]{2,1,0:T(8,128)(2,1)S(1)} %get-tuple-element.89), channel_id=1, source_target_pairs={{0,5},{1,4},{2,7},{3,6},{4,1},{5,0},{6,3},{7,2},{8,13},{9,12},{10,... | collective-permute-start | bytes 393224 | tf_op jit(solution)/shard_map/ppermute | solution.py:63
  9.3 6.6 %collective-permute-start.2 = (bf16[2,64,512]{2,1,0:T(8,128)(2,1)S(1)}, bf16[2,64,512]{2,1,0:T(8,128)(2,1)S(1)}, u32[]{:S(2)}, u32[]{:S(2)}) collective-permute-start(bf16[2,64,512]{2,1,0:T(8,128)(2,1)S(1)} %get-tuple-element.87), channel_id=1, source_target_pairs={{0,4},{1,5},{2,6},{3,7},{4,0},{5,1},{6,2},{7,3},{8,12},{9,13},{10,... | collective-permute-start | bytes 393224 | tf_op jit(solution)/shard_map/ppermute | solution.py:63
  9.8 6.4 %collective-permute-start.3 = (bf16[2,64,512]{2,1,0:T(8,128)(2,1)S(1)}, bf16[2,64,512]{2,1,0:T(8,128)(2,1)S(1)}, u32[]{:S(2)}, u32[]{:S(2)}) collective-permute-start(bf16[2,64,512]{2,1,0:T(8,128)(2,1)S(1)} %get-tuple-element.88), channel_id=1, source_target_pairs={{0,1},{1,0},{2,3},{3,2},{4,5},{5,4},{6,7},{7,6},{8,9},{9,8},{10,11... | collective-permute-start | bytes 393224 | tf_op jit(solution)/shard_map/ppermute | solution.py:63
  16.3 5.2 %collective-permute-start.4 = (bf16[2,64,512]{2,1,0:T(8,128)(2,1)S(1)}, bf16[2,64,512]{2,1,0:T(8,128)(2,1)S(1)}, u32[]{:S(2)}, u32[]{:S(2)}) collective-permute-start(bf16[2,64,512]{2,1,0:T(8,128)(2,1)S(1)} %fusion.4), channel_id=1, source_target_pairs={{0,8},{1,9},{2,10},{3,11},{4,12},{5,13},{6,14},{7,15},{8,0},{9,1},... | collective-permute-start | bytes 393224 | tf_op jit(solution)/shard_map/ppermute | solution.py:63
  18.0 22.9 %copy-start.4 = (f32[4096,128]{1,0:T(8,128)S(1)}, f32[4096,128]{1,0:T(8,128)}, u32[]{:S(2)}) copy-start(f32[4096,128]{1,0:T(8,128)} %coef_ref.3) | copy-start | bytes 6291460
  21.6 8.5 %collective-permute-start.5 = (bf16[2,64,512]{2,1,0:T(8,128)(2,1)S(1)}, bf16[2,64,512]{2,1,0:T(8,128)(2,1)S(1)}, u32[]{:S(2)}, u32[]{:S(2)}) collective-permute-start(bf16[2,64,512]{2,1,0:T(8,128)(2,1)S(1)} %broadcast_select_fusion.9), channel_id=1, source_target_pairs={{0,16},{1,17},{2,18},{3,19},{4,20},{5,21},{6,22},{7,23},{8,24},{9,... | collective-permute-start | bytes 393224 | tf_op jit(solution)/shard_map/ppermute | solution.py:63
  30.2 6.9 %collective-permute-start.6 = (bf16[2,64,512]{2,1,0:T(8,128)(2,1)S(1)}, bf16[2,64,512]{2,1,0:T(8,128)(2,1)S(1)}, u32[]{:S(2)}, u32[]{:S(2)}) collective-permute-start(bf16[2,64,512]{2,1,0:T(8,128)(2,1)S(1)} %broadcast_select_fusion.10), channel_id=1, source_target_pairs={{0,5},{1,4},{2,7},{3,6},{4,1},{5,0},{6,3},{7,2},{8,13},{9,12},{10,... | collective-permute-start | bytes 393224 | tf_op jit(solution)/shard_map/ppermute | solution.py:63
  31.3 7.1 %collective-permute-start.7 = (bf16[2,64,512]{2,1,0:T(8,128)(2,1)S(1)}, bf16[2,64,512]{2,1,0:T(8,128)(2,1)S(1)}, u32[]{:S(2)}, u32[]{:S(2)}) collective-permute-start(bf16[2,64,512]{2,1,0:T(8,128)(2,1)S(1)} %broadcast_select_fusion.10), channel_id=1, source_target_pairs={{0,4},{1,5},{2,6},{3,7},{4,0},{5,1},{6,2},{7,3},{8,12},{9,13},{10,... | collective-permute-start | bytes 393224 | tf_op jit(solution)/shard_map/ppermute | solution.py:63
  33.2 5.3 %collective-permute-start.8 = (bf16[2,64,512]{2,1,0:T(8,128)(2,1)S(1)}, bf16[2,64,512]{2,1,0:T(8,128)(2,1)S(1)}, u32[]{:S(2)}, u32[]{:S(2)}) collective-permute-start(bf16[2,64,512]{2,1,0:T(8,128)(2,1)S(1)} %broadcast_select_fusion.10), channel_id=1, source_target_pairs={{0,1},{1,0},{2,3},{3,2},{4,5},{5,4},{6,7},{7,6},{8,9},{9,8},{10,11... | collective-permute-start | bytes 393224 | tf_op jit(solution)/shard_map/ppermute | solution.py:63
  38.6 2.0 %collective-permute-start.9 = (bf16[2,4,64,512]{3,2,1,0:T(8,128)(2,1)S(1)}, bf16[2,4,64,512]{3,2,1,0:T(8,128)(2,1)S(1)}, u32[]{:S(2)}, u32[]{:S(2)}) collective-permute-start(bf16[2,4,64,512]{3,2,1,0:T(8,128)(2,1)S(1)} %pad_maximum_fusion.1), channel_id=1, source_target_pairs={{0,2},{1,3},{2,0},{3,1},{4,6},{5,7},{6,4},{7,5},{8,10},{9,11},{10,... | collective-permute-start | bytes 1572872 | tf_op jit(solution)/shard_map/ppermute | solution.py:63
  58.8 2.5 %collective-permute-start.10 = (f32[2,2,96,512]{3,2,1,0:T(8,128)S(1)}, f32[2,2,96,512]{3,2,1,0:T(8,128)}, u32[]{:S(2)}, u32[]{:S(2)}) collective-permute-start(f32[2,2,96,512]{3,2,1,0:T(8,128)S(1)} %select_bitcast_fusion), channel_id=1, source_target_pairs={{0,2},{1,3},{2,0},{3,1},{4,6},{5,7},{6,4},{7,5},{8,10},{9,11},{10,... | collective-permute-start | bytes 2359304 | tf_op jit(solution)/shard_map/ppermute | solution.py:63
  62.7 68.2 %collective-permute-start.11 = (f32[96,512]{1,0:T(8,128)S(1)}, f32[96,512]{1,0:T(8,128)S(1)}, u32[]{:S(2)}, u32[]{:S(2)}) collective-permute-start(f32[96,512]{1,0:T(8,128)S(1)} %get-tuple-element.80), channel_id=1, source_target_pairs={{0,1},{1,0},{2,3},{3,2},{4,5},{5,4},{6,7},{7,6},{8,9},{9,8},{10,11... | collective-permute-start | bytes 589832 | tf_op jit(solution)/shard_map/ppermute | solution.py:63
  64.2 66.8 %collective-permute-start.12 = (f32[96,512]{1,0:T(8,128)S(1)}, f32[96,512]{1,0:T(8,128)S(1)}, u32[]{:S(2)}, u32[]{:S(2)}) collective-permute-start(f32[96,512]{1,0:T(8,128)S(1)} %get-tuple-element.79), channel_id=1, source_target_pairs={{0,4},{1,5},{2,6},{3,7},{4,0},{5,1},{6,2},{7,3},{8,12},{9,13},{10,... | collective-permute-start | bytes 589832 | tf_op jit(solution)/shard_map/ppermute | solution.py:63
  64.8 66.2 %collective-permute-start.13 = (f32[96,512]{1,0:T(8,128)S(1)}, f32[96,512]{1,0:T(8,128)S(1)}, u32[]{:S(2)}, u32[]{:S(2)}) collective-permute-start(f32[96,512]{1,0:T(8,128)S(1)} %get-tuple-element.78), channel_id=1, source_target_pairs={{0,5},{1,4},{2,7},{3,6},{4,1},{5,0},{6,3},{7,2},{8,13},{9,12},{10,... | collective-permute-start | bytes 589832 | tf_op jit(solution)/shard_map/ppermute | solution.py:63
  131.1 7.8 %collective-permute-start.14 = (f32[96,512]{1,0:T(8,128)S(1)}, f32[96,512]{1,0:T(8,128)S(1)}, u32[]{:S(2)}, u32[]{:S(2)}) collective-permute-start(f32[96,512]{1,0:T(8,128)S(1)} %fusion.3), channel_id=1, source_target_pairs={{0,8},{1,9},{2,10},{3,11},{4,12},{5,13},{6,14},{7,15},{8,0},{9,1},... | collective-permute-start | bytes 589832 | tf_op jit(solution)/shard_map/ppermute | solution.py:63
  138.7 23.0 %collective-permute-start.20 = (f32[256,512]{1,0:T(8,128)S(1)}, f32[256,512]{1,0:T(8,128)S(1)}, u32[]{:S(2)}, u32[]{:S(2)}) collective-permute-start(f32[256,512]{1,0:T(8,128)S(1)} %get-tuple-element.57), channel_id=1, source_target_pairs={{0,2},{1,3},{2,0},{3,1},{4,6},{5,7},{6,4},{7,5},{8,10},{9,11},{10,... | collective-permute-start | bytes 1572872 | tf_op jit(solution)/shard_map/ppermute | solution.py:63
  138.9 12.7 %collective-permute-start.15 = (f32[96,512]{1,0:T(8,128)S(1)}, f32[96,512]{1,0:T(8,128)S(1)}, u32[]{:S(2)}, u32[]{:S(2)}) collective-permute-start(f32[96,512]{1,0:T(8,128)S(1)} %add.54), channel_id=1, source_target_pairs={{0,16},{1,17},{2,18},{3,19},{4,20},{5,21},{6,22},{7,23},{8,24},{9,... | collective-permute-start | bytes 589832 | tf_op jit(solution)/shard_map/ppermute | solution.py:63
  148.6 13.3 %collective-permute-start.21 = (f32[256,512]{1,0:T(8,128)S(1)}, f32[256,512]{1,0:T(8,128)S(1)}, u32[]{:S(2)}, u32[]{:S(2)}) collective-permute-start(f32[256,512]{1,0:T(8,128)S(1)} %get-tuple-element.58), channel_id=1, source_target_pairs={{0,2},{1,3},{2,0},{3,1},{4,6},{5,7},{6,4},{7,5},{8,10},{9,11},{10,... | collective-permute-start | bytes 1572872 | tf_op jit(solution)/shard_map/ppermute | solution.py:63
  151.6 9.3 %collective-permute-start.16 = (bf16[64,512]{1,0:T(8,128)(2,1)S(1)}, bf16[64,512]{1,0:T(8,128)(2,1)S(1)}, u32[]{:S(2)}, u32[]{:S(2)}) collective-permute-start(bf16[64,512]{1,0:T(8,128)(2,1)S(1)} %slice.26), channel_id=1, source_target_pairs={{0,1},{1,0},{2,3},{3,2},{4,5},{5,4},{6,7},{7,6},{8,9},{9,8},{10,11... | collective-permute-start | bytes 196616 | tf_op jit(solution)/shard_map/ppermute | solution.py:63
  153.0 8.0 %collective-permute-start.17 = (bf16[64,512]{1,0:T(8,128)(2,1)S(1)}, bf16[64,512]{1,0:T(8,128)(2,1)S(1)}, u32[]{:S(2)}, u32[]{:S(2)}) collective-permute-start(bf16[64,512]{1,0:T(8,128)(2,1)S(1)} %slice.26), channel_id=1, source_target_pairs={{0,4},{1,5},{2,6},{3,7},{4,0},{5,1},{6,2},{7,3},{8,12},{9,13},{10,... | collective-permute-start | bytes 196616 | tf_op jit(solution)/shard_map/ppermute | solution.py:63
  153.6 7.4 %collective-permute-start.18 = (bf16[64,512]{1,0:T(8,128)(2,1)S(1)}, bf16[64,512]{1,0:T(8,128)(2,1)S(1)}, u32[]{:S(2)}, u32[]{:S(2)}) collective-permute-start(bf16[64,512]{1,0:T(8,128)(2,1)S(1)} %slice.26), channel_id=1, source_target_pairs={{0,5},{1,4},{2,7},{3,6},{4,1},{5,0},{6,3},{7,2},{8,13},{9,12},{10,... | collective-permute-start | bytes 196616 | tf_op jit(solution)/shard_map/ppermute | solution.py:63
  160.9 3.3 %collective-permute-start.22 = (f32[256,512]{1,0:T(8,128)S(1)}, f32[256,512]{1,0:T(8,128)S(1)}, u32[]{:S(2)}, u32[]{:S(2)}) collective-permute-start(f32[256,512]{1,0:T(8,128)S(1)} %get-tuple-element.59), channel_id=1, source_target_pairs={{0,2},{1,3},{2,0},{3,1},{4,6},{5,7},{6,4},{7,5},{8,10},{9,11},{10,... | collective-permute-start | bytes 1572872 | tf_op jit(solution)/shard_map/ppermute | solution.py:63
  161.0 3.3 %collective-permute-start.23 = (f32[256,512]{1,0:T(8,128)S(1)}, f32[256,512]{1,0:T(8,128)S(1)}, u32[]{:S(2)}, u32[]{:S(2)}) collective-permute-start(f32[256,512]{1,0:T(8,128)S(1)} %factor.7), channel_id=1, source_target_pairs={{0,2},{1,3},{2,0},{3,1},{4,6},{5,7},{6,4},{7,5},{8,10},{9,11},{10,... | collective-permute-start | bytes 1572872 | tf_op jit(solution)/shard_map/ppermute | solution.py:63
  161.6 2.4 %collective-permute-start.19 = (bf16[2,2,64,512]{3,2,1,0:T(8,128)(2,1)S(1)}, bf16[2,2,64,512]{3,2,1,0:T(8,128)(2,1)S(1)}, u32[]{:S(2)}, u32[]{:S(2)}) collective-permute-start(bf16[2,2,64,512]{3,2,1,0:T(8,128)(2,1)S(1)} %bitcast.111), channel_id=1, source_target_pairs={{0,2},{1,3},{2,0},{3,1},{4,6},{5,7},{6,4},{7,5},{8,10},{9,11},{10,... | collective-permute-start | bytes 786440 | tf_op jit(solution)/shard_map/ppermute | solution.py:63
  164.1 11.7 %slice-start = ((s8[8388608]{0:T(1024)(128)(4,1)}), s8[4194304]{0:T(1024)(128)(4,1)S(1)}, s32[]{:S(2)}) async-start(s8[8388608]{0:T(1024)(128)(4,1)} %bitcast.98), calls=%async_computation | async-start | bytes 8388608
  164.4 11.3 %slice-start.1 = ((s8[8388608]{0:T(1024)(128)(4,1)}), s8[4194304]{0:T(1024)(128)(4,1)S(1)}, s32[]{:S(2)}) async-start(s8[8388608]{0:T(1024)(128)(4,1)} %bitcast.98), calls=%async_computation.1 | async-start | bytes 8388608
  165.6 10.1 %copy-start.3 = (f32[4096,128]{1,0:T(8,128)S(1)}, f32[4096,128]{1,0:T(8,128)}, u32[]{:S(2)}) copy-start(f32[4096,128]{1,0:T(8,128)} %res_ref.3) | copy-start | bytes 6291460
  167.4 4.8 %collective-permute-start.24 = (bf16[32,512]{1,0:T(8,128)(2,1)S(1)}, bf16[32,512]{1,0:T(8,128)(2,1)S(1)}, u32[]{:S(2)}, u32[]{:S(2)}) collective-permute-start(bf16[32,512]{1,0:T(8,128)(2,1)S(1)} %second.1), channel_id=1, source_target_pairs={{0,5},{1,4},{2,7},{3,6},{4,1},{5,0},{6,3},{7,2},{8,13},{9,12},{10,... | collective-permute-start | bytes 98312 | tf_op jit(solution)/shard_map/ppermute | solution.py:63
  168.8 3.9 %collective-permute-start.25 = (bf16[32,512]{1,0:T(8,128)(2,1)S(1)}, bf16[32,512]{1,0:T(8,128)(2,1)S(1)}, u32[]{:S(2)}, u32[]{:S(2)}) collective-permute-start(bf16[32,512]{1,0:T(8,128)(2,1)S(1)} %second.1), channel_id=1, source_target_pairs={{0,4},{1,5},{2,6},{3,7},{4,0},{5,1},{6,2},{7,3},{8,12},{9,13},{10,... | collective-permute-start | bytes 98312 | tf_op jit(solution)/shard_map/ppermute | solution.py:63
  170.3 3.9 %collective-permute-start.26 = (bf16[32,512]{1,0:T(8,128)(2,1)S(1)}, bf16[32,512]{1,0:T(8,128)(2,1)S(1)}, u32[]{:S(2)}, u32[]{:S(2)}) collective-permute-start(bf16[32,512]{1,0:T(8,128)(2,1)S(1)} %second.1), channel_id=1, source_target_pairs={{0,1},{1,0},{2,3},{3,2},{4,5},{5,4},{6,7},{7,6},{8,9},{9,8},{10,11... | collective-permute-start | bytes 98312 | tf_op jit(solution)/shard_map/ppermute | solution.py:63
  174.3 1.4 collective-permute-start.27
  (7 other events, 31.7 us)
